TPU v7x, 32 devices: a whole 2x2x4 slice. The times are simulated.
32 devices in a mesh: dp: 8 (over z, y), seq: 4 (over x, core).
Axes of the slice: x: 2, y: 2, z: 4, core: 2. Of those that a mesh axis runs over, the one named last changes fastest.
Arguments:
- tokens: bfloat16 [8, 2048, 1024], P('dp', 'seq'), may hold values from -6 to 6
- positions: int32 [3, 8, 2048], P(None, 'dp', 'seq'), may hold values from 0 to 15, as said below
- adapter_index: int32 [8, 1], P('dp'), may hold values from 0 to 7
- qkv_weight: bfloat16 [1024, 3072], P('dp', 'seq'), may hold values from -0.1875 to 0.1875
- proj_weight: bfloat16 [1024, 1024], P('dp', 'seq'), may hold values from -0.75 to 0.75
- fc1_weight: bfloat16 [1024, 4096], P('dp', 'seq'), may hold values from -0.1875 to 0.1875
- fc2_weight: bfloat16 [4096, 1024], P('dp', 'seq'), may hold values from -0.09375 to 0.09375
- vectors: bfloat16 [9, 1024], P(None, 'seq')
- fc1_bias: bfloat16 [4096], P('seq'), may hold values from -3 to 3
- adapter_down: bfloat16 [8, 16, 7168], P(None, 'dp', 'seq'), may hold values from -0.1875 to 0.1875
- adapter_up: bfloat16 [8, 16, 9216], P(None, 'dp', 'seq'), may hold values from -1.5 to 1.5
- cotangent: bfloat16 [8, 2048, 1024], P('dp', 'seq'), may hold values from -6 to 6
Outputs:
- output: bfloat16 [8, 2048, 1024], P('dp', 'seq')
- input_grad: bfloat16 [8, 2048, 1024], P('dp', 'seq')
- down_grad: float32 [8, 16, 7168], P(None, 'dp', 'seq')
- up_grad: float32 [8, 16, 9216], P(None, 'dp', 'seq')
Inputs may be any that keep to these rules, and one draw needn't show every extreme that they name: `adapter_index`: every adapter is used by at least one clip. `positions`: each clip's tokens sit on 2048 distinct cells of a grid of 16 frames by 16 rows by 16 columns, in raster order (frame, then row, then column); every clip holds the last cell of the grid.
All inputs are finite; a program needn't handle non-finite values.
Results may differ from a plain program's by a relative error of at most 0.019.
Values may be sent and summed in bfloat16 or wider, within the bound.
A program may use at most 320 MiB of HBM per device.

v0:
```python
import math

import jax
import jax.numpy as jnp
from jax import lax
from jax.sharding import PartitionSpec as P

D = 1024
HEADS = 16
HD = 64
FF = 4096
NA = 8


def layer_norm(values, gain_row, shift_row):
    centre = values - jnp.mean(values, axis=-1, keepdims=True)
    spread = jnp.mean(centre * centre, axis=-1, keepdims=True)
    return centre * lax.rsqrt(spread + 1e-06) * gain_row + shift_row


def rotate(values, places, direction):
    rot_span = 2 * (values.shape[-1] // 3 // 2)
    half_span = rot_span // 2
    inverse_freq = 10000.0 ** (-jnp.arange(half_span, dtype=jnp.float32) / half_span)
    pieces = []
    for axis_id in range(3):
        segment = values[..., axis_id * rot_span : (axis_id + 1) * rot_span]
        angles = places[axis_id].astype(jnp.float32)[..., None, None] * inverse_freq
        cosine = jnp.cos(angles)
        sine_wave = direction * jnp.sin(angles)
        lower_part = segment[..., :half_span]
        upper_part = segment[..., half_span:]
        pieces.append(lower_part * cosine - upper_part * sine_wave)
        pieces.append(lower_part * sine_wave + upper_part * cosine)
    pieces.append(values[..., 3 * rot_span :])
    return jnp.concatenate(pieces, axis=-1)


def exact_gelu(values):
    return jax.nn.gelu(values, approximate=False)


def fetch_weight(weight):
    joined = lax.all_gather(weight, "seq", axis=1, tiled=True)
    return lax.all_gather(joined, "dp", axis=0, tiled=True)


def adapted(inputs, weight, shift_row, down_part, up_part):
    base = jnp.einsum("cti,io->cto", inputs, weight, preferred_element_type=jnp.float32)
    reduced = jnp.einsum(
        "cti,cri->ctr", inputs, down_part, preferred_element_type=jnp.float32
    ).astype(jnp.bfloat16)
    result = (
        base
        + shift_row
        + jnp.einsum("ctr,cro->cto", reduced, up_part, preferred_element_type=jnp.float32)
    )
    return (result, reduced)


def adapted_back(grad_out, inputs, weight, down_part, up_part, reduced):
    grad_in = jnp.einsum("cto,io->cti", grad_out, weight, preferred_element_type=jnp.float32)
    grad_reduced = jnp.einsum(
        "cto,cro->ctr", grad_out, up_part, preferred_element_type=jnp.float32
    ).astype(jnp.bfloat16)
    grad_in = grad_in + jnp.einsum(
        "ctr,cri->cti", grad_reduced, down_part, preferred_element_type=jnp.float32
    )
    grad_down = jnp.einsum("ctr,cti->cri", grad_reduced, inputs, preferred_element_type=jnp.float32)
    grad_up = jnp.einsum("ctr,cto->cro", reduced, grad_out, preferred_element_type=jnp.float32)
    return (grad_in, grad_down, grad_up)


def split_tokens(source, split_count):
    old_shape = source.shape
    shaped = source.reshape(
        (old_shape[0], split_count, old_shape[1] // split_count) + old_shape[2:]
    )
    return jnp.moveaxis(shaped, 1, 0)


def score_grads(
    query_block, key_block, value_block, grad_block, log_block, delta_block, score_scale
):
    scores = (
        jnp.einsum("cqhd,ckhd->chqk", query_block, key_block, preferred_element_type=jnp.float32)
        * score_scale
    )
    probabilities = jnp.exp(scores - log_block[..., None])
    grad_probs = jnp.einsum(
        "cqhd,ckhd->chqk", grad_block, value_block, preferred_element_type=jnp.float32
    )
    grad_scores = (probabilities * (grad_probs - delta_block[..., None])).astype(jnp.bfloat16)
    return (probabilities.astype(jnp.bfloat16), grad_scores)


def shards(
    tokens,
    positions,
    adapter_index,
    qkv_weight,
    proj_weight,
    fc1_weight,
    fc2_weight,
    vectors,
    fc1_bias,
    adapter_down,
    adapter_up,
    cotangent,
):
    clip_count, tok_count = (tokens.shape[0], tokens.shape[1])
    head_shape = (clip_count, tok_count, HEADS, HD)
    score_scale = HD ** (-0.5)
    small_parts = (
        lax.all_gather(adapter_down, "seq", axis=2, tiled=True),
        lax.all_gather(adapter_up, "seq", axis=2, tiled=True),
        lax.all_gather(vectors, "seq", axis=1, tiled=True),
        lax.all_gather(fc1_bias, "seq", axis=0, tiled=True),
    )
    down_all, up_all = (
        lax.all_gather(small_parts[0], "dp", axis=1, tiled=True),
        lax.all_gather(small_parts[1], "dp", axis=1, tiled=True),
    )
    vector_rows = small_parts[2].astype(jnp.float32)
    hidden_bias = small_parts[3].astype(jnp.float32)
    choose = (adapter_index == jnp.arange(NA, dtype=jnp.int32)[None, :]).astype(jnp.bfloat16)
    down_sel = jnp.einsum(
        "ca,ari->cri", choose, down_all, preferred_element_type=jnp.float32
    ).astype(jnp.bfloat16)
    up_sel = jnp.einsum("ca,aro->cro", choose, up_all, preferred_element_type=jnp.float32).astype(
        jnp.bfloat16
    )
    down_parts = (
        down_sel[:, :, :D],
        down_sel[:, :, D : 2 * D],
        down_sel[:, :, 2 * D : 3 * D],
        down_sel[:, :, 3 * D :],
    )
    up_parts = (
        up_sel[:, :, : 3 * D],
        up_sel[:, :, 3 * D : 4 * D],
        up_sel[:, :, 4 * D : 4 * D + FF],
        up_sel[:, :, 4 * D + FF :],
    )
    inputs = tokens.astype(jnp.float32)
    normed_one = layer_norm(inputs, vector_rows[0], vector_rows[1]).astype(jnp.bfloat16)
    weight_qkv = fetch_weight(qkv_weight)
    mixed_qkv, reduced_qkv = adapted(
        normed_one, weight_qkv, vector_rows[4:7].reshape(3 * D), down_parts[0], up_parts[0]
    )
    queries = rotate(mixed_qkv[..., :D].reshape(head_shape), positions, 1.0).astype(jnp.bfloat16)
    keys_local = rotate(mixed_qkv[..., D : 2 * D].reshape(head_shape), positions, 1.0).astype(
        jnp.bfloat16
    )
    values_local = mixed_qkv[..., 2 * D :].reshape(head_shape).astype(jnp.bfloat16)
    stat_shape = (clip_count, HEADS, tok_count)
    start_state = (
        jnp.full(stat_shape, -jnp.inf, jnp.float32),
        jnp.zeros(stat_shape, jnp.float32),
        jnp.zeros(stat_shape + (HD,), jnp.float32),
    )
    key_piece = lax.all_gather(keys_local, "seq", axis=1, tiled=True)
    value_piece = lax.all_gather(values_local, "seq", axis=1, tiled=True)
    split_count = key_piece.shape[1] // math.gcd(key_piece.shape[1], 256)

    def inner_step(running, block_pair):
        top_score, row_total, weighted = running
        key_block, value_block = block_pair
        scores = (
            jnp.einsum("cqhd,ckhd->chqk", queries, key_block, preferred_element_type=jnp.float32)
            * score_scale
        )
        new_top = jnp.maximum(top_score, jnp.max(scores, axis=-1))
        factor = jnp.exp(top_score - new_top)
        weights = jnp.exp(scores - new_top[..., None])
        row_total = row_total * factor + jnp.sum(weights, axis=-1)
        weighted = weighted * factor[..., None] + jnp.einsum(
            "chqk,ckhd->chqd",
            weights.astype(jnp.bfloat16),
            value_block,
            preferred_element_type=jnp.float32,
        )
        return ((new_top, row_total, weighted), None)

    result, unused = lax.scan(
        inner_step,
        start_state,
        (split_tokens(key_piece, split_count), split_tokens(value_piece, split_count)),
    )
    top_score, row_total, weighted = result
    log_total = top_score + jnp.log(row_total)
    heads_tok = jnp.swapaxes(weighted / row_total[..., None], 1, 2)
    attended = heads_tok.reshape(clip_count, tok_count, D).astype(jnp.bfloat16)
    weight_proj = fetch_weight(proj_weight)
    projected, reduced_proj = adapted(
        attended, weight_proj, vector_rows[7], down_parts[1], up_parts[1]
    )
    residual = inputs + projected
    normed_two = layer_norm(residual, vector_rows[2], vector_rows[3]).astype(jnp.bfloat16)
    weight_up = fetch_weight(fc1_weight)
    hidden, reduced_up = adapted(normed_two, weight_up, hidden_bias, down_parts[2], up_parts[2])
    activated = exact_gelu(hidden).astype(jnp.bfloat16)
    weight_down = fetch_weight(fc2_weight)
    branch, reduced_down = adapted(
        activated, weight_down, vector_rows[8], down_parts[3], up_parts[3]
    )
    output = (residual + branch).astype(jnp.bfloat16)
    weight_down = fetch_weight(fc2_weight)
    grad_act, gdown_four, gup_four = adapted_back(
        cotangent, activated, weight_down, down_parts[3], up_parts[3], reduced_down
    )
    unused, gelu_back = jax.vjp(exact_gelu, hidden)
    grad_hidden = gelu_back(grad_act)[0].astype(jnp.bfloat16)
    weight_up = fetch_weight(fc1_weight)
    grad_normed_two, gdown_three, gup_three = adapted_back(
        grad_hidden, normed_two, weight_up, down_parts[2], up_parts[2], reduced_up
    )

    def norm_two(values):
        return layer_norm(values, vector_rows[2], vector_rows[3])

    unused, norm_two_back = jax.vjp(norm_two, residual)
    grad_residual = cotangent.astype(jnp.float32) + norm_two_back(grad_normed_two)[0]
    weight_proj = fetch_weight(proj_weight)
    grad_attended, gdown_two, gup_two = adapted_back(
        grad_residual.astype(jnp.bfloat16),
        attended,
        weight_proj,
        down_parts[1],
        up_parts[1],
        reduced_proj,
    )
    grad_tok = grad_attended.astype(jnp.bfloat16).reshape(head_shape)
    delta_heads = jnp.swapaxes(jnp.sum(grad_tok.astype(jnp.float32) * heads_tok, axis=-1), 1, 2)
    whole_keys, whole_values = (
        lax.all_gather(keys_local, "seq", axis=1, tiled=True),
        lax.all_gather(values_local, "seq", axis=1, tiled=True),
    )
    block_count = whole_keys.shape[1] // math.gcd(whole_keys.shape[1], 256)
    key_blocks = split_tokens(whole_keys, block_count)
    value_blocks = split_tokens(whole_values, block_count)
    zero_heads = jnp.zeros(head_shape, jnp.float32)

    def back_step(grad_query, block_pair):
        key_block, value_block = block_pair
        probs_low, grad_scores = score_grads(
            queries, key_block, value_block, grad_tok, log_total, delta_heads, score_scale
        )
        grad_query = (
            grad_query
            + jnp.einsum(
                "chqk,ckhd->cqhd", grad_scores, key_block, preferred_element_type=jnp.float32
            )
            * score_scale
        )
        grad_key = (
            jnp.einsum("chqk,cqhd->ckhd", grad_scores, queries, preferred_element_type=jnp.float32)
            * score_scale
        )
        grad_value = jnp.einsum(
            "chqk,cqhd->ckhd", probs_low, grad_tok, preferred_element_type=jnp.float32
        )
        return (grad_query, jnp.concatenate([grad_key, grad_value], axis=-1))

    grad_query, key_terms = lax.scan(back_step, zero_heads, (key_blocks, value_blocks))
    key_terms = jnp.moveaxis(key_terms, 0, 1).reshape(
        clip_count, whole_keys.shape[1], HEADS, 2 * HD
    )
    summed = lax.psum_scatter(
        key_terms.astype(jnp.bfloat16), "seq", scatter_dimension=1, tiled=True
    ).astype(jnp.float32)
    grad_key = summed[..., :HD]
    grad_value = summed[..., HD:]
    grad_mixed = jnp.concatenate(
        [
            rotate(grad_query, positions, -1.0).reshape(clip_count, tok_count, D),
            rotate(grad_key, positions, -1.0).reshape(clip_count, tok_count, D),
            grad_value.reshape(clip_count, tok_count, D),
        ],
        axis=-1,
    ).astype(jnp.bfloat16)
    weight_qkv = fetch_weight(qkv_weight)
    grad_normed_one, gdown_one, gup_one = adapted_back(
        grad_mixed, normed_one, weight_qkv, down_parts[0], up_parts[0], reduced_qkv
    )

    def norm_one(values):
        return layer_norm(values, vector_rows[0], vector_rows[1])

    unused, norm_one_back = jax.vjp(norm_one, inputs)
    input_grad = (grad_residual + norm_one_back(grad_normed_one)[0]).astype(jnp.bfloat16)
    choose_wide = choose.astype(jnp.float32)
    clip_down = jnp.concatenate([gdown_one, gdown_two, gdown_three, gdown_four], axis=-1)
    clip_up = jnp.concatenate([gup_one, gup_two, gup_three, gup_four], axis=-1)
    down_term = jnp.einsum("ca,cri->ari", choose_wide, clip_down, precision=lax.Precision.HIGHEST)
    up_term = jnp.einsum("ca,cro->aro", choose_wide, clip_up, precision=lax.Precision.HIGHEST)
    down_grad, up_grad = (
        lax.psum_scatter(
            down_term.astype(jnp.bfloat16), "seq", scatter_dimension=2, tiled=True
        ).astype(jnp.float32),
        lax.psum_scatter(
            up_term.astype(jnp.bfloat16), "seq", scatter_dimension=2, tiled=True
        ).astype(jnp.float32),
    )
    down_grad, up_grad = (
        lax.psum_scatter(
            down_grad.astype(jnp.bfloat16), "dp", scatter_dimension=1, tiled=True
        ).astype(jnp.float32),
        lax.psum_scatter(
            up_grad.astype(jnp.bfloat16), "dp", scatter_dimension=1, tiled=True
        ).astype(jnp.float32),
    )
    return (output, input_grad, down_grad, up_grad)


def solution(mesh):
    in_specs = (
        P("dp", "seq", None),
        P(None, "dp", "seq"),
        P("dp", None),
        P("dp", "seq"),
        P("dp", "seq"),
        P("dp", "seq"),
        P("dp", "seq"),
        P(None, "seq"),
        P("seq"),
        P(None, "dp", "seq"),
        P(None, "dp", "seq"),
        P("dp", "seq", None),
    )
    out_specs = (
        P("dp", "seq", None),
        P("dp", "seq", None),
        P(None, "dp", "seq"),
        P(None, "dp", "seq"),
    )
    return jax.shard_map(shards, mesh=mesh, in_specs=in_specs, out_specs=out_specs, check_vma=False)
```

profile of v0, /device:TPU:0, one launch (start us, length us, event | category | flops | bytes accessed | tf_op | source)
XLA Modules:
  0.0 1187.4 jit_solution(2797440207636428401)
XLA Ops:
  8.8 7.5 all_gather.61
  17.3 7.6 all_gather.63
  24.9 11.4 all_gather.59
  46.9 32.3 %all-gather.13.cloned.1.call-done = bf16[8,16,7168]{2,0,1:T(8,128)(2,1)} async-done(((bf16[8,2,7168]{2,0,1:T(8,128)(2,1)}), bf16[8,16,7168]{2,0,1:T(8,128)(2,1)}) %all-gather.13.cloned.1.call-update) | async-done | bytes 1835024 | tf_op jit(solution)/shard_map/all_gather | solution.py:121
  81.8 50.7 %all-gather.15.cloned.1.call-done = bf16[8,16,9216]{2,0,1:T(8,128)(2,1)} async-done(((bf16[8,2,9216]{2,0,1:T(8,128)(2,1)}), bf16[8,16,9216]{2,0,1:T(8,128)(2,1)}) %all-gather.15.cloned.1.call-update) | async-done | bytes 2359312 | tf_op jit(solution)/shard_map/all_gather | solution.py:122
  135.1 97.1 %all-gather.11.cloned.1.call-done = bf16[1024,3072]{1,0:T(8,128)(2,1)} async-done(((bf16[128,3072]{1,0:T(8,128)(2,1)}), bf16[1024,3072]{1,0:T(8,128)(2,1)}) %all-gather.11.cloned.1.call-update) | async-done | bytes 6291472 | tf_op jit(solution)/shard_map/all_gather | solution.py:45
  248.6 19.7 %concatenate.56 = bf16[1,512,16,64]{1,3,2,0:T(8,128)(2,1)} concatenate(bf16[1,512,16,10]{1,3,2,0:T(8,128)(2,1)} %get-tuple-element.282, bf16[1,512,16,10]{1,3,2,0:T(8,128)(2,1)} %get-tuple-element.283, bf16[1,512,16,10]{1,3,2,0:T(8,128)(2,1)S(1)} %get-tuple-element.280, bf16[1,512,16,10]{1,3,2,0:T(8,128)(2,1)S(1)} %get-tuple-element.281, ...), dimensions={3} | concatenate | bytes 2097152 | tf_op jit(solution)/shard_map/concatenate | solution.py:36
  271.5 6.3 all_gather.67
  293.1 14.7 %concatenate.57 = bf16[1,512,16,64]{1,3,2,0:T(8,128)(2,1)S(1)} concatenate(bf16[1,512,16,10]{1,3,2,0:T(8,128)(2,1)} %get-tuple-element.278, bf16[1,512,16,10]{1,3,2,0:T(8,128)(2,1)} %get-tuple-element.279, bf16[1,512,16,10]{1,3,2,0:T(8,128)(2,1)} %get-tuple-element.276, bf16[1,512,16,10]{1,3,2,0:T(8,128)(2,1)} %get-tuple-element.277, ...), dimensions={3} | concatenate | bytes 2097152 | tf_op jit(solution)/shard_map/concatenate | solution.py:36
  307.8 67.6 %all-gather.29.cloned.1.call-done = bf16[4096,1024]{1,0:T(8,128)(2,1)} async-done(((bf16[512,1024]{1,0:T(8,128)(2,1)}), bf16[4096,1024]{1,0:T(8,128)(2,1)}) %all-gather.29.cloned.1.call-update) | async-done | bytes 8388624 | tf_op jit(solution)/shard_map/all_gather | solution.py:45
  375.5 11.7 fusion.67
  387.1 23.2 %all-gather.17.cloned.1.call-done = bf16[1,2048,16,64]{1,3,2,0:T(8,128)(2,1)} async-done(((bf16[1,512,16,64]{1,3,2,0:T(8,128)(2,1)}), bf16[1,2048,16,64]{1,3,2,0:T(8,128)(2,1)}) %all-gather.17.cloned.1.call-update) | async-done | bytes 4194320 | tf_op jit(solution)/shard_map/all_gather | solution.py:162
  415.0 31.9 %all-gather.19.cloned.1.call-done = bf16[1,2048,16,64]{1,3,2,0:T(8,128)(2,1)} async-done(((bf16[1,512,16,64]{1,3,2,0:T(8,128)(2,1)}), bf16[1,2048,16,64]{1,3,2,0:T(8,128)(2,1)}) %all-gather.19.cloned.1.call-update) | async-done | bytes 4194320 | tf_op jit(solution)/shard_map/all_gather | solution.py:163
  451.7 117.4 %while.28 = (s32[]{:T(128)}, f32[1,16,512]{2,1,0:T(8,128)S(1)}, f32[1,16,512]{2,1,0:T(8,128)S(1)}, f32[1,16,512,64]{2,3,1,0:T(8,128)S(1)}, bf16[8,1,256,16,64]{2...) while((s32[]{:T(128)}, f32[1,16,512]{2,1,0:T(8,128)S(1)}, ...), condition=%wide.region_5.6_spmd.clone, body=%wide.region_2.5_spmd.clone.sunk | while | flops 555270144 | bytes 65536148 | solution.py:185
  466.2 5.6 bitcast_reduce_fusion.2
  524.8 5.6 bitcast_reduce_fusion.2
  539.3 5.6 bitcast_reduce_fusion.2
  578.6 45.3 %all-gather.25.cloned.1.call-done = bf16[1024,4096]{1,0:T(8,128)(2,1)} async-done(((bf16[128,4096]{1,0:T(8,128)(2,1)}), bf16[1024,4096]{1,0:T(8,128)(2,1)}) %all-gather.25.cloned.1.call-update) | async-done | bytes 8388624 | tf_op jit(solution)/shard_map/all_gather | solution.py:45
  623.8 7.3 fusion.93
  631.2 21.3 %multiply_convert_fusion.1 = (bf16[512,4096]{1,0:T(8,128)(2,1)}, f32[512,4096]{1,0:T(8,128)}, f32[512,4096]{1,0:T(8,128)}) fusion(bf16[512,16]{0,1:T(8,128)(2,1)S(1)} %convolution_convert_fusion.4, bf16[1,16,9216]{2,1,0:T(8,128)(2,1)S(1)} %copy.89, f32[512,4096]{1,0:T(8,128)S(1)} %fusion.93, f32[4096]{0:T(1024)S(1)} %copy-done.82), kind=kOutput, calls=%fused_computation.54 | convolution fusion | flops 207618048 | bytes 29523968 | tf_op jit(solution)/shard_map/ctr,cro->cto/dot_general | solution.py:56
  652.6 10.5 add_convert_fusion
  678.2 194.2 %while.29 = (s32[]{:T(128)}, f32[1,512,16,64]{1,3,2,0:T(8,128)}, bf16[8,1,256,16,128]{4,3,2,0,1:T(8,128)(2,1)}, bf16[8,1,256,16,64]{2,4,3,1,0:T(8,128)(2,1)}, bf...) while((s32[]{:T(128)}, f32[1,512,16,64]{1,3,2,0:T(8,128)}, ...), condition=%wide.region_12.13_spmd.clone, body=%wide.region_11.12_spmd.clone.sunk | while | flops 1363148800 | bytes 139034864 | solution.py:265
  872.4 12.5 %copy.58 = bf16[1,2048,16,128]{1,3,2,0:T(8,128)(2,1)} copy(bf16[1,2048,16,128]{3,2,1,0:T(8,128)(2,1)} %bitcast.341) | data formatting | bytes 16777216 | tf_op jit(solution)/shard_map/convert_element_type | solution.py:270
  889.9 21.9 %concatenate.58 = bf16[1,512,16,64]{1,3,2,0:T(8,128)(2,1)} concatenate(bf16[1,512,16,10]{1,3,2,0:T(8,128)(2,1)} %get-tuple-element.274, bf16[1,512,16,10]{1,3,2,0:T(8,128)(2,1)} %get-tuple-element.275, bf16[1,512,16,10]{1,3,2,0:T(8,128)(2,1)} %get-tuple-element.272, bf16[1,512,16,10]{1,3,2,0:T(8,128)(2,1)} %get-tuple-element.273, bf16[1,512,16,10]{1,3,2,0:T(8,128)(2,1)} %get-tuple-element.255, ...), dimensions={3} | concatenate | bytes 2097152 | tf_op jit(solution)/shard_map/concatenate | solution.py:36
  922.3 32.7 %reduce-scatter.6.cloned.1.call-done = bf16[1,512,16,128]{1,3,2,0:T(8,128)(2,1)} async-done(((bf16[1,2048,16,128]{1,3,2,0:T(8,128)(2,1)}), bf16[1,512,16,128]{1,3,2,0:T(8,128)(2,1)}) %reduce-scatter.6.cloned.1.call-update) | async-done | bytes 2097168 | tf_op jit(solution)/shard_map/reduce_scatter | solution.py:269
  958.9 19.7 %concatenate.60 = bf16[1,512,16,64]{1,3,2,0:T(8,128)(2,1)} concatenate(bf16[1,512,16,10]{1,3,2,0:T(8,128)(2,1)} %get-tuple-element.252, bf16[1,512,16,10]{1,3,2,0:T(8,128)(2,1)} %get-tuple-element.253, bf16[1,512,16,10]{1,3,2,0:T(8,128)(2,1)S(1)} %get-tuple-element.250, bf16[1,512,16,10]{1,3,2,0:T(8,128)(2,1)S(1)} %get-tuple-element.251, ...), dimensions={3} | concatenate | bytes 2097152 | tf_op jit(solution)/shard_map/concatenate | solution.py:36
  990.5 8.7 fusion.94
  1000.7 12.8 %reduce-scatter.8.cloned.1.call-done = bf16[8,16,1792]{2,1,0:T(8,128)(2,1)} async-done(((bf16[8,16,7168]{2,1,0:T(8,128)(2,1)}), bf16[8,16,1792]{2,1,0:T(8,128)(2,1)}) %reduce-scatter.8.cloned.1.call-update) | async-done | bytes 458768 | tf_op jit(solution)/shard_map/reduce_scatter | solution.py:298
  1015.5 7.3 fusion.85
  1022.9 26.2 %reduce-scatter.12.cloned.1.call-done = bf16[8,16,2304]{2,1,0:T(8,128)(2,1)} async-done(((bf16[8,16,9216]{2,1,0:T(8,128)(2,1)}), bf16[8,16,2304]{2,1,0:T(8,128)(2,1)}) %reduce-scatter.12.cloned.1.call-update) | async-done | bytes 589840 | tf_op jit(solution)/shard_map/reduce_scatter | solution.py:301
  1055.4 59.1 %reduce-scatter.10.cloned.1.call-done = bf16[8,2,1792]{2,0,1:T(8,128)(2,1)} async-done(((bf16[8,16,1792]{2,0,1:T(8,128)(2,1)}), bf16[8,2,1792]{2,0,1:T(8,128)(2,1)}) %reduce-scatter.10.cloned.1.call-update) | async-done | bytes 57360 | tf_op jit(solution)/shard_map/reduce_scatter | solution.py:306
  1116.0 62.8 %reduce-scatter.14.cloned.1.call-done = bf16[8,2,2304]{2,0,1:T(8,128)(2,1)} async-done(((bf16[8,16,2304]{2,0,1:T(8,128)(2,1)}), bf16[8,2,2304]{2,0,1:T(8,128)(2,1)}) %reduce-scatter.14.cloned.1.call-update) | async-done | bytes 73744 | tf_op jit(solution)/shard_map/reduce_scatter | solution.py:309
  (476 shorter events, 423.2 us)
Async XLA Ops:
  7.2 36.3 %copy-start.8 = (bf16[1,512,1024]{2,1,0:T(8,128)(2,1)S(1)}, bf16[1,512,1024]{2,1,0:T(8,128)(2,1)}, u32[]{:S(2)}) copy-start(bf16[1,512,1024]{2,1,0:T(8,128)(2,1)} %param.16) | copy-start | bytes 3145732
  7.2 37.5 %copy-start.86 = (s32[3,1,512]{2,1,0:T(1,128)S(1)}, s32[3,1,512]{2,1,0:T(1,128)}, u32[]{:S(2)}) copy-start(s32[3,1,512]{2,1,0:T(1,128)} %param.17) | copy-start | bytes 18436
  7.2 29.8 %all-gather.27.cloned.1.call-start = ((), (), s32[]{:S(2)}) async-start(), calls=%async_computation.13 | async-start | bytes 1310720 | tf_op jit(solution)/shard_map/all_gather | solution.py:44
  7.9 71.3 %all-gather.13.cloned.1.call-start = ((), (), s32[]{:S(2)}) async-start(), calls=%async_computation.6 | async-start | bytes 2064384 | tf_op jit(solution)/shard_map/all_gather | solution.py:121
  16.3 116.2 %all-gather.15.cloned.1.call-start = ((), (), s32[]{:S(2)}) async-start(), calls=%async_computation.7 | async-start | bytes 2654208 | tf_op jit(solution)/shard_map/all_gather | solution.py:122
  24.9 207.3 %all-gather.11.cloned.1.call-start = ((), (), s32[]{:S(2)}) async-start(), calls=%async_computation.5 | async-start | bytes 7077888 | tf_op jit(solution)/shard_map/all_gather | solution.py:45
  36.3 247.4 %all-gather.23.cloned.1.call-start = ((), (), s32[]{:S(2)}) async-start(), calls=%async_computation.11 | async-start | bytes 1310720 | tf_op jit(solution)/shard_map/all_gather | solution.py:44
  36.9 338.5 %all-gather.29.cloned.1.call-start = ((), (), s32[]{:S(2)}) async-start(), calls=%async_computation.14 | async-start | bytes 9437184 | tf_op jit(solution)/shard_map/all_gather | solution.py:45
  37.5 372.8 %all-gather.17.cloned.1.call-start = ((), (), s32[]{:S(2)}) async-start(), calls=%async_computation.8 | async-start | bytes 5242880 | tf_op jit(solution)/shard_map/all_gather | solution.py:162
  43.7 91.3 %copy-start.58 = (f32[512]{0:T(512)}, f32[512]{0:T(512)S(1)}, u32[]{:S(2)}) copy-start(f32[512]{0:T(512)S(1)} %broadcast_multiply_fusion.4) | copy-start | bytes 6148
  44.7 90.3 %copy-start.73 = (f32[512]{0:T(512)}, f32[512]{0:T(512)S(1)}, u32[]{:S(2)}) copy-start(f32[512]{0:T(512)S(1)} %fusion.75) | copy-start | bytes 6148
  45.3 89.7 %copy-start.71 = (f32[1,1024]{1,0:T(1,128)}, f32[1,1024]{1,0:T(1,128)S(1)}, u32[]{:S(2)}) copy-start(f32[1,1024]{1,0:T(1,128)S(1)} %get-tuple-element.288) | copy-start | bytes 12292
  46.4 199.9 %copy-start.38 = (f32[512,10]{0,1:T(8,128)}, f32[512,10]{0,1:T(8,128)S(1)}, u32[]{:S(2)}) copy-start(f32[512,10]{0,1:T(8,128)S(1)} %get-tuple-element.303) | copy-start | bytes 61444
  46.4 199.9 %copy-start.41 = (f32[512,10]{0,1:T(8,128)}, f32[512,10]{0,1:T(8,128)S(1)}, u32[]{:S(2)}) copy-start(f32[512,10]{0,1:T(8,128)S(1)} %get-tuple-element.305) | copy-start | bytes 61444
  46.4 241.0 %copy-start.36 = (f32[512,10]{0,1:T(8,128)}, f32[512,10]{0,1:T(8,128)S(1)}, u32[]{:S(2)}) copy-start(f32[512,10]{0,1:T(8,128)S(1)} %get-tuple-element.294) | copy-start | bytes 61444
  46.8 190.8 %copy-start.22 = (bf16[512,1024]{1,0:T(8,128)(2,1)}, bf16[512,1024]{1,0:T(8,128)(2,1)S(1)}, u32[]{:S(2)}) copy-start(bf16[512,1024]{1,0:T(8,128)(2,1)S(1)} %fusion.64) | copy-start | bytes 3145732
  81.4 51.1 %copy-start.29 = (bf16[1,16,7168]{2,1,0:T(8,128)(2,1)}, bf16[1,16,7168]{2,1,0:T(8,128)(2,1)S(1)}, u32[]{:S(2)}) copy-start(bf16[1,16,7168]{2,1,0:T(8,128)(2,1)S(1)} %copy.90) | copy-start | bytes 688132
  81.8 155.9 %copy-start.60 = (bf16[512,16]{0,1:T(8,128)(2,1)}, bf16[512,16]{0,1:T(8,128)(2,1)S(1)}, u32[]{:S(2)}) copy-start(bf16[512,16]{0,1:T(8,128)(2,1)S(1)} %convolution_convert_fusion.5) | copy-start | bytes 49156
  268.3 178.7 %all-gather.19.cloned.1.call-start = ((), (), s32[]{:S(2)}) async-start(), calls=%async_computation.9 | async-start | bytes 5242880 | tf_op jit(solution)/shard_map/all_gather | solution.py:163
  271.5 300.2 %all-gather.21.cloned.1.call-start = ((), (), s32[]{:S(2)}) async-start(), calls=%async_computation.10 | async-start | bytes 2359296 | tf_op jit(solution)/shard_map/all_gather | solution.py:45
  277.8 346.0 %all-gather.25.cloned.1.call-start = ((), (), s32[]{:S(2)}) async-start(), calls=%async_computation.12 | async-start | bytes 9437184 | tf_op jit(solution)/shard_map/all_gather | solution.py:45
  283.7 671.2 %reduce-scatter.6.cloned.1.call-start = ((), (), s32[]{:S(2)}) async-start(), calls=%async_computation.15 | async-start | bytes 10485760 | tf_op jit(solution)/shard_map/reduce_scatter | solution.py:269
  284.4 368.2 %copy-start.62 = (bf16[16,512]{1,0:T(8,128)(2,1)}, bf16[16,512]{1,0:T(8,128)(2,1)S(1)}, u32[]{:S(2)}) copy-start(bf16[16,512]{1,0:T(8,128)(2,1)S(1)} %convolution_convert_fusion.3) | copy-start | bytes 49156
  575.6 94.0 %copy-start.6 = (f32[1,512,1024]{2,1,0:T(8,128)}, f32[1,512,1024]{2,1,0:T(8,128)S(1)}, u32[]{:S(2)}) copy-start(f32[1,512,1024]{2,1,0:T(8,128)S(1)} %get-tuple-element.309) | copy-start | bytes 6291460
  575.7 93.1 %copy-start.69 = (f32[512]{0:T(512)}, f32[512]{0:T(512)S(1)}, u32[]{:S(2)}) copy-start(f32[512]{0:T(512)S(1)} %broadcast_multiply_fusion.3) | copy-start | bytes 6148
  576.0 55.2 %copy-start.77 = (f32[512]{0:T(512)}, f32[512]{0:T(512)S(1)}, u32[]{:S(2)}) copy-start(f32[512]{0:T(512)S(1)} %fusion.76) | copy-start | bytes 6148
  578.6 52.6 %copy-start.64 = (bf16[512,16]{0,1:T(8,128)(2,1)}, bf16[512,16]{0,1:T(8,128)(2,1)S(1)}, u32[]{:S(2)}) copy-start(bf16[512,16]{0,1:T(8,128)(2,1)S(1)} %convolution_convert_fusion.4) | copy-start | bytes 49156
  623.8 40.4 %slice-start = ((s8[8388608]{0:T(1024)(128)(4,1)}), s8[4194304]{0:T(1024)(128)(4,1)S(1)}, s32[]{:S(2)}) async-start(s8[8388608]{0:T(1024)(128)(4,1)} %bitcast.371), calls=%async_computation.20 | async-start | bytes 8388608
  884.9 128.5 %reduce-scatter.8.cloned.1.call-start = ((), (), s32[]{:S(2)}) async-start(), calls=%async_computation.16 | async-start | bytes 2293760 | tf_op jit(solution)/shard_map/reduce_scatter | solution.py:298
  983.5 65.6 %reduce-scatter.12.cloned.1.call-start = ((), (), s32[]{:S(2)}) async-start(), calls=%async_computation.18 | async-start | bytes 2949120 | tf_op jit(solution)/shard_map/reduce_scatter | solution.py:301
  990.5 124.0 %reduce-scatter.10.cloned.1.call-start = ((), (), s32[]{:S(2)}) async-start(), calls=%async_computation.17 | async-start | bytes 516096 | tf_op jit(solution)/shard_map/reduce_scatter | solution.py:306
  1015.5 163.3 %reduce-scatter.14.cloned.1.call-start = ((), (), s32[]{:S(2)}) async-start(), calls=%async_computation.19 | async-start | bytes 663552 | tf_op jit(solution)/shard_map/reduce_scatter | solution.py:309
  (103 other events, 792.9 us)
Sparse Core Ops, SparseCore 0:
  9.6 20.0 all-gather.26
  31.9 47.2 all-gather.12
  81.4 51.1 all-gather.14
  134.6 97.5 all-gather.10
  233.6 14.9 all-gather.22
  250.5 124.8 all-gather.28
  377.6 32.6 all-gather.16
  412.4 34.4 all-gather.18
  449.1 49.2 all-gather.20
  500.4 123.4 all-gather.24
  885.0 69.8 reduce-scatter.5
  983.6 29.8 reduce-scatter.7
  1016.0 33.0 reduce-scatter.11
  1052.6 61.8 reduce-scatter.9
  1117.6 61.0 reduce-scatter.13
where the time goes:
time: 1200 us; the launch traced here: 1190 us
  waiting for transfers between devices  544 us (45%)
  matrix products  306 us (26%)
  local copies, waits for them, and re-layouts  201 us (17%)
  other arithmetic  75.6 us (6%)
  blocking collectives  43.1 us (4%)
  between operations  16.3 us (1%)
    all_gather x4, waiting for transfers between devices, fetch_weight(): return lax.all_gather(joined, 'dp', axis=0, tiled=True)  210 us
    concatenate x4, local copies, waits for them, and re-layouts, rotate(): return jnp.concatenate(pieces, axis=-1)  76 us
    reduce_scatter x1, waiting for transfers between devices, shards(): lax.psum_scatter(up_grad.astype(jnp.bfloat16), 'dp', scatter_dimension=1,...  62.8 us
    reduce_scatter x1, waiting for transfers between devices, shards(): lax.psum_scatter(down_grad.astype(jnp.bfloat16), 'dp', scatter_dimension=...  59.1 us
    all_gather x1, waiting for transfers between devices, shards(): lax.all_gather(small_parts[1], 'dp', axis=1, tiled=True)  50.7 us
    while x72, local copies, waits for them, and re-layouts  45.8 us
    dot_general x8, matrix products, inner_step(): jnp.einsum('cqhd,ckhd->chqk', queries, key_block, preferred_element_type=...  45.1 us
    dot_general x8, matrix products, back_step(): jnp.einsum('chqk,ckhd->cqhd', grad_scores, key_block, preferred_element_t...  41.7 us
  transfers between devices with their start and end apart: 15, of which 12 were waited for; matrix products, arithmetic and copies ran while one was open for 23% of the time, Pallas kernels for 0%

commit v1 on v0

--- a/solution.py
+++ b/solution.py
@@ -1,8 +1,11 @@
+import functools
 import math
 
 import jax
 import jax.numpy as jnp
 from jax import lax
+from jax.experimental import pallas as pl
+from jax.experimental.pallas import tpu as pltpu
 from jax.sharding import PartitionSpec as P
 
 D = 1024
@@ -312,6 +315,738 @@
     )
     return (output, input_grad, down_grad, up_grad)
 
+MESH = pl.DeviceIdType.MESH
+BF = jnp.bfloat16
+F32 = jnp.float32
+LOG2E = 1.4426950408889634
+LN2 = 0.6931471805599453
+VM = 60 * 1024 * 1024
+
+
+def mm(a, b):
+    return lax.dot_general(a, b, (((1,), (0,)), ((), ())), preferred_element_type=F32)
+
+
+def mm_nt(a, b):
+    return lax.dot_general(a, b, (((1,), (1,)), ((), ())), preferred_element_type=F32)
+
+
+def mm_tn(a, b):
+    return lax.dot_general(a, b, (((0,), (0,)), ((), ())), preferred_element_type=F32)
+
+
+class Links:
+    def __init__(self, ssem, rsem, lsem, nz):
+        self.ssem, self.rsem, self.lsem = ssem, rsem, lsem
+        self.nr, self.nl = 0, 0
+        d, s = lax.axis_index("dp"), lax.axis_index("seq")
+        self.d, self.s, self.nz = d, s, nz
+        self.z, self.y, self.x, self.c = d // 2, lax.rem(d, 2), s // 2, lax.rem(s, 2)
+        self.core = (d, s + 1 - 2 * self.c)
+        self.xn = (d, s + 2 - 4 * self.x)
+        self.diag = (d, 3 - s)
+        self.yn = (d + 1 - 2 * self.y, s)
+        self.up, self.down = (d + 2, s), (d - 2, s)
+        self.tail = []
+
+    def barrier(self):
+        bar = pltpu.get_barrier_semaphore()
+        for dev in (self.core, self.xn, self.yn):
+            pl.semaphore_signal(bar, inc=1, device_id=dev, device_id_type=MESH)
+
+        @pl.when(self.z < self.nz - 1)
+        def _():
+            pl.semaphore_signal(bar, inc=1, device_id=self.up, device_id_type=MESH)
+
+        @pl.when(self.z > 0)
+        def _():
+            pl.semaphore_signal(bar, inc=1, device_id=self.down, device_id_type=MESH)
+
+        edge = (self.z == 0).astype(jnp.int32) + (self.z == self.nz - 1).astype(jnp.int32)
+        pl.semaphore_wait(bar, 5 - edge)
+
+    def new(self, count=1):
+        self.nr += count
+        return self.nr - count
+
+    def newl(self):
+        self.nl += 1
+        return self.nl - 1
+
+    def remote(self, i, src, dst, dev):
+        return pltpu.make_async_remote_copy(
+            src_ref=src,
+            dst_ref=dst,
+            send_sem=self.ssem.at[i],
+            recv_sem=self.rsem.at[i],
+            device_id=dev,
+            device_id_type=MESH,
+        )
+
+    def local(self, i, src, dst):
+        return pltpu.make_async_copy(src, dst, self.lsem.at[i])
+
+
+def guard(cond, body):
+    if cond is None:
+        body()
+    else:
+        pl.when(cond)(body)
+
+
+class Part:
+    def __init__(self, links, order, own, region, handover):
+        self.k, self.order, self.own = links, order, own
+        self.region, self.handover = region, handover
+        k = links
+        self.s_own = k.newl()
+        self.s_up, self.s_dn = k.new(k.nz - 1), k.new(k.nz - 1)
+        self.s_f, self.s_g1, self.s_g2 = k.new(), k.new(), k.new()
+        self.pend = []
+        self.steps = self.steps_zlast() if order == "xyz" else self.steps_zfirst()
+
+    def reg(self, fi, gi, zs):
+        return self.region(fi, zs, gi) if self.order == "zxy" else self.region(gi, zs, fi)
+
+    def hand(self, cond, x, zs, y):
+        k = self.k
+        loc, rem = self.handover(x, zs, y)
+        ls = [(k.newl(), a, b) for a, b in loc]
+        rs = [(k.new(), a, b, w) for a, b, w in rem]
+
+        def start():
+            for i, a, b in ls:
+                k.local(i, a, b).start()
+            for i, a, b, _ in rs:
+                k.remote(i, a, b, k.core).start()
+
+        def finish():
+            for i, a, b in ls:
+                k.local(i, a, b).wait()
+            for i, a, b, w in rs:
+                k.remote(i, a, w, k.core).wait_recv()
+                k.remote(i, a, b, k.core).wait_send()
+
+        guard(cond, start)
+        self.pend.append((cond, finish))
+
+    def line(self, src, at, zs_hand, first_hand):
+        k = self.k
+        z, nz = k.z, k.nz
+        can_up, can_dn = z < nz - 1, z > 0
+        guard(can_up, lambda: k.remote(self.s_up, src, at(z), k.up).start())
+        guard(can_dn, lambda: k.remote(self.s_dn, src, at(z), k.down).start())
+        k.tail.append((can_up, lambda: k.remote(self.s_up, src, at(z), k.up).wait_send()))
+        k.tail.append((can_dn, lambda: k.remote(self.s_dn, src, at(z), k.down).wait_send()))
+        yield
+        for r in range(nz - 1):
+            for sem, here, origin, dev, can in (
+                (self.s_up, z > r, z - 1 - r, k.up, can_up),
+                (self.s_dn, z + r < nz - 1, z + 1 + r, k.down, can_dn),
+            ):
+                guard(
+                    here,
+                    lambda: k.remote(sem + r, at(origin), at(origin), dev).wait_recv(),
+                )
+                if r < nz - 2:
+                    go = jnp.logical_and(here, can)
+                    guard(
+                        go, lambda: k.remote(sem + r + 1, at(origin), at(origin), dev).start()
+                    )
+                    k.tail.append(
+                        (
+                            go,
+                            lambda sem=sem, r=r, origin=origin, dev=dev: k.remote(
+                                sem + r + 1, at(origin), at(origin), dev
+                            ).wait_send(),
+                        )
+                    )
+                if zs_hand is not None:
+                    zs_hand(here, origin)
+            if r < nz - 2:
+                yield
+
+    def steps_zfirst(self):
+        k = self.k
+        f, g = (k.x, k.y) if self.order == "zxy" else (k.y, k.x)
+        fd, gd = (k.xn, k.yn) if self.order == "zxy" else (k.yn, k.xn)
+        xy = (lambda a, b: (a, b)) if self.order == "zxy" else (lambda a, b: (b, a))
+        al = slice(None)
+
+        def hand(a, b):
+            x, y = xy(a, b)
+            self.hand(None, x, al, y)
+
+        own_copy = k.local(self.s_own, self.own, self.reg(f, g, k.z))
+        own_copy.start()
+        yield from self.line(self.own, lambda z: self.reg(f, g, z), None, None)
+        own_copy.wait()
+        mine, nf = self.reg(f, g, al), self.reg(1 - f, g, al)
+        ng, nfg = self.reg(f, 1 - g, al), self.reg(1 - f, 1 - g, al)
+        c_f = k.remote(self.s_f, mine, mine, fd)
+        c_g1 = k.remote(self.s_g1, mine, mine, gd)
+        c_g2 = k.remote(self.s_g2, nf, nf, gd)
+        c_f.start()
+        c_g1.start()
+        hand(f, g)
+        yield
+        k.remote(self.s_f, mine, nf, fd).wait_recv()
+        c_g2.start()
+        hand(1 - f, g)
+        yield
+        k.remote(self.s_g1, mine, ng, gd).wait_recv()
+        hand(f, 1 - g)
+        yield
+        k.remote(self.s_g2, nf, nfg, gd).wait_recv()
+        hand(1 - f, 1 - g)
+        for cp in (c_f, c_g1, c_g2):
+            k.tail.append((None, cp.wait_send))
+        yield
+
+    def steps_zlast(self):
+        k = self.k
+        x, y, z = k.x, k.y, k.z
+        al = slice(None)
+        own_copy = k.local(self.s_own, self.own, self.region(x, z, y))
+        own_copy.start()
+        c_f = k.remote(self.s_f, self.own, self.region(x, z, y), k.xn)
+        c_g1 = k.remote(self.s_g1, self.own, self.region(x, z, y), k.yn)
+        c_f.start()
+        c_g1.start()
+        yield
+        k.remote(self.s_f, self.own, self.region(1 - x, z, y), k.xn).wait_recv()
+        c_g2 = k.remote(self.s_g2, self.region(1 - x, z, y), self.region(1 - x, z, y), k.yn)
+        c_g2.start()
+        yield
+        k.remote(self.s_g1, self.own, self.region(x, z, 1 - y), k.yn).wait_recv()
+        k.remote(
+            self.s_g2, self.region(1 - x, z, y), self.region(1 - x, z, 1 - y), k.yn
+        ).wait_recv()
+        own_copy.wait()
+        for cp in (c_f, c_g1, c_g2):
+            k.tail.append((None, cp.wait_send))
+        self.hand(None, al, z, al)
+        yield from self.line(
+            self.region(al, z, al),
+            lambda o: self.region(al, o, al),
+            lambda here, o: self.hand(here, al, o, al),
+            None,
+        )
+        yield
+
+    def finish(self):
+        for cond, body in self.pend:
+            guard(cond, body)
+
+
+def wide_parts(links, shard, buf, cuts):
+    c = links.c
+    parts = []
+    for r0, n, order in cuts:
+        rows = pl.ds(r0, n)
+
+        def region(x, z, y, rows=rows):
+            return buf.at[x, c, z, y, rows]
+
+        def handover(x, z, y, rows=rows):
+            at = buf.at[x, c, z, y, rows]
+            return [], [(at, at, buf.at[x, 1 - c, z, y, rows])]
+
+        parts.append(Part(links, order, shard.at[rows], region, handover))
+    return parts
+
+
+def qkv_parts(links, shard, lane, buf, cuts):
+    c = links.c
+    parts = []
+    for r0, n, order in cuts:
+        rows = pl.ds(r0, n)
+
+        def region(x, z, y, rows=rows):
+            return lane.at[x, z, y, rows]
+
+        def handover(x, z, y, rows=rows):
+            loc, rem = [], []
+            for xx in (0, 1) if isinstance(x, slice) else (x,):
+                for col, role in ((0, 3 * xx + c), (512, 3 * xx + c + 1)):
+                    loc.append((lane.at[xx, z, y, rows, pl.ds(col, 256)], buf.at[role, z, y, rows]))
+                rem.append(
+                    (
+                        lane.at[xx, z, y, rows, pl.ds(256, 256)],
+                        buf.at[3 * xx + 2 * c, z, y, rows],
+                        buf.at[3 * xx + 2 - 2 * c, z, y, rows],
+                    )
+                )
+            return loc, rem
+
+        parts.append(Part(links, order, shard.at[rows], region, handover))
+    return parts
+
+
+def wavefront(steps):
+    steps = list(steps)
+    live = []
+    while steps or live:
+        if steps:
+            live.append(steps.pop(0))
+        for gen in list(live):
+            try:
+                next(gen)
+            except StopIteration:
+                live.remove(gen)
+
+
+def gather_kernel(nz, tok, qkv, proj, fc1, fc2, tok4, lane, wq, wp, w1, w2, ssem, rsem, lsem):
+    k = Links(ssem, rsem, lsem, nz)
+    k.barrier()
+    i_own, i_core, i_x, i_d = k.newl(), k.new(), k.new(), k.new()
+    own = k.local(i_own, tok, tok4.at[0])
+    own.start()
+    to_core = k.remote(i_core, tok, tok4.at[1], k.core)
+    to_x = k.remote(i_x, tok, tok4.at[2], k.xn)
+    to_core.start()
+    to_x.start()
+    parts = (
+        qkv_parts(k, qkv, lane, wq, ((0, 80, "zxy"), (80, 48, "xyz")))
+        + wide_parts(k, proj, wp, ((0, 128, "zyx"),))
+        + wide_parts(k, fc1, w1, ((0, 96, "zxy"), (96, 32, "zyx")))
+        + wide_parts(k, fc2, w2, ((0, 256, "zxy"), (256, 256, "xyz")))
+    )
+
+    def tokens():
+        yield
+        yield
+        yield
+        to_x.wait_recv()
+        fwd = k.remote(i_d, tok4.at[2], tok4.at[3], k.core)
+        fwd.start()
+        yield
+        fwd.wait()
+
+    wavefront([p.steps for p in parts[:2]] + [tokens()] + [p.steps for p in parts[2:]])
+    for p in parts:
+        p.finish()
+    own.wait()
+    to_core.wait()
+    to_x.wait_send()
+    for cond, body in k.tail:
+        guard(cond, body)
+
+
+def gather_all(nz, tok, qkv, proj, fc1, fc2):
+    anyspec = pl.BlockSpec(memory_space=pl.ANY)
+    out = [
+        jax.ShapeDtypeStruct((4,) + tok.shape, BF),
+        jax.ShapeDtypeStruct((2, nz, 2) + qkv.shape, BF),
+        jax.ShapeDtypeStruct((6, nz, 2, qkv.shape[0], 256), BF),
+    ] + [jax.ShapeDtypeStruct((2, 2, nz, 2) + w.shape, BF) for w in (proj, fc1, fc2)]
+    return pl.pallas_call(
+        functools.partial(gather_kernel, nz),
+        out_shape=out,
+        in_specs=[anyspec] * 5,
+        out_specs=[anyspec] * 6,
+        scratch_shapes=[
+            pltpu.SemaphoreType.DMA((160,)),
+            pltpu.SemaphoreType.DMA((160,)),
+            pltpu.SemaphoreType.DMA((64,)),
+        ],
+        compiler_params=pltpu.CompilerParams(collective_id=0, has_side_effects=True),
+    )(tok, qkv, proj, fc1, fc2)
+
+
+def norm_parts(values):
+    centre = values - jnp.mean(values, axis=-1, keepdims=True)
+    inv = lax.rsqrt(jnp.mean(centre * centre, axis=-1, keepdims=True) + 1e-06)
+    return centre * inv, inv
+
+
+def swap_pairs(v):
+    n = v.shape[1]
+    j = lax.rem(lax.broadcasted_iota(jnp.int32, (1, n), 1), HD)
+    lower = lax.rem(j, 20) < 10
+    return jnp.where(lower, pltpu.roll(v, n - 10, 1), pltpu.roll(v, 10, 1))
+
+
+def turn(v, cos, sin):
+    cc, ss = jnp.concatenate([cos, cos], axis=1), jnp.concatenate([sin, sin], axis=1)
+    return v * cc + swap_pairs(v) * ss
+
+
+def qkv_body(tok4, tab, wq, down, up6, bias6, gain, shift, n1, red, q, k, v):
+    for slot in range(4):
+        xhat, _ = norm_parts(tok4[slot].astype(F32))
+        h = (xhat * gain[...] + shift[...]).astype(BF)
+        n1[slot] = h
+        low = mm_nt(h, down[...]).astype(BF)
+        red[slot] = low
+        cos, sin = tab[slot, :, :128], tab[slot, :, 128:]
+        rows = pl.ds(slot * 512, 512)
+        for role in range(0 if slot < 2 else 2, 6):
+            val = mm(h, wq[role]) + bias6[role] + mm(low, up6[role])
+            cols = pl.ds((role % 2) * 256, 256)
+            if role < 2:
+                q[rows, cols] = (turn(val, cos, sin) * (LOG2E * HD**-0.5)).astype(BF)
+            elif role < 4:
+                k[rows, cols] = turn(val, cos, sin).astype(BF)
+            else:
+                v[rows, cols] = val.astype(BF)
+
+
+def attend_body(q_ref, k_ref, v_ref, o_ref, l_ref):
+    lane = lax.broadcasted_iota(jnp.int32, (1, 128), 1)
+    ks, qs = k_ref[...], q_ref[...]
+    vt = v_ref[...].T
+    outs = []
+    for e in range(2):
+        keep = (lane < 64) if e == 0 else (lane >= 64)
+        st = mm_nt(ks, jnp.where(keep, qs, jnp.zeros_like(qs)))
+        top = jnp.max(st, axis=0, keepdims=True)
+        pr = jnp.exp2(st - top)
+        total = jnp.sum(pr, axis=0, keepdims=True)
+        outs.append(mm(vt[64 * e : 64 * e + 64], pr.astype(BF)) / total)
+        l_ref[e : e + 1, :] = top + jnp.log2(total)
+    o_ref[...] = jnp.concatenate(outs, axis=0).T.astype(BF)
+
+
+def attend(q, k, v):
+    nq, nk = q.shape[0], k.shape[0]
+    qb = min(1024, nq)
+    return pl.pallas_call(
+        attend_body,
+        grid=(4, nq // qb),
+        in_specs=[
+            pl.BlockSpec((qb, 128), lambda h, i: (i, h)),
+            pl.BlockSpec((nk, 128), lambda h, i: (0, h)),
+            pl.BlockSpec((nk, 128), lambda h, i: (0, h)),
+        ],
+        out_specs=[
+            pl.BlockSpec((qb, 128), lambda h, i: (i, h)),
+            pl.BlockSpec((None, 2, qb), lambda h, i: (h, 0, i)),
+        ],
+        out_shape=[
+            jax.ShapeDtypeStruct((nq, 512), BF),
+            jax.ShapeDtypeStruct((4, 2, nq), F32),
+        ],
+        compiler_params=pltpu.CompilerParams(vmem_limit_bytes=VM),
+    )(q, k, v)
+
+
+def attend_back_body(q_ref, do_ref, o_ref, k_ref, v_ref, lse_ref, dq_ref, dk_ref, dv_ref, acc, dl):
+    lane = lax.broadcasted_iota(jnp.int32, (1, 128), 1)
+    kb = pl.program_id(1)
+    q, do, ks, vs = q_ref[...], do_ref[...], k_ref[...], v_ref[...]
+
+    @pl.when(kb == 0)
+    def _():
+        prod = do.astype(F32) * o_ref[...].astype(F32)
+        r8 = lax.broadcasted_iota(jnp.int32, (8, 128), 0)
+        l8 = lax.broadcasted_iota(jnp.int32, (8, 128), 1) // 64
+        pick = (r8 == l8).astype(F32)
+        dl[...] = lax.dot_general(
+            pick,
+            prod,
+            (((1,), (1,)), ((), ())),
+            precision=lax.Precision.HIGHEST,
+            preferred_element_type=F32,
+        )
+
+    dks, dvs, dqs = [], [], []
+    for e in range(2):
+        keep = (lane < 64) if e == 0 else (lane >= 64)
+        st = mm_nt(jnp.where(keep, ks, jnp.zeros_like(ks)), q)
+        pr = jnp.exp2(st - lse_ref[e : e + 1, :])
+        dp = mm_nt(jnp.where(keep, vs, jnp.zeros_like(vs)), do)
+        ds = (pr * (dp - dl[e : e + 1, :])).astype(BF)
+        dvs.append(mm(pr.astype(BF), do))
+        dks.append(mm(ds, q))
+        dqs.append(mm(ks.T[64 * e : 64 * e + 64], ds))
+    dk_ref[...] = jnp.where(lane < 64, dks[0], dks[1]) * LN2
+    dv_ref[...] = jnp.where(lane < 64, dvs[0], dvs[1])
+    dq = jnp.concatenate(dqs, axis=0)
+
+    @pl.when(kb == 0)
+    def _():
+        acc[...] = dq
+
+    @pl.when(kb > 0)
+    def _():
+        acc[...] += dq
+
+    @pl.when(kb == pl.num_programs(1) - 1)
+    def _():
+        dq_ref[...] = acc[...].T * (HD**-0.5)
+
+
+def attend_back(q, do, o, k, v, lse):
+    nq, nk = q.shape[0], k.shape[0]
+    kb = 1024
+    full = pl.BlockSpec((nq, 128), lambda h, i: (0, h))
+    part = pl.BlockSpec((kb, 128), lambda h, i: (i, h))
+    return pl.pallas_call(
+        attend_back_body,
+        grid=(4, nk // kb),
+        in_specs=[full, full, full, part, part, pl.BlockSpec((None, 2, nq), lambda h, i: (h, 0, 0))],
+        out_specs=[full, part, part],
+        out_shape=[
+            jax.ShapeDtypeStruct((nq, 512), F32),
+            jax.ShapeDtypeStruct((nk, 512), F32),
+            jax.ShapeDtypeStruct((nk, 512), F32),
+        ],
+        scratch_shapes=[pltpu.VMEM((128, nq), F32), pltpu.VMEM((8, nq), F32)],
+        compiler_params=pltpu.CompilerParams(vmem_limit_bytes=VM),
+    )(q, do, o, k, v, lse)
+
+
+def norm_back(grad, xhat, inv, gain):
+    q = grad * gain
+    return inv * (
+        q - jnp.mean(q, axis=-1, keepdims=True) - xhat * jnp.mean(q * xhat, axis=-1, keepdims=True)
+    )
+
+
+def ffn_body(
+    att, tok, cot, wp, w1, w2, dp_, d1, d2, up, u1, u2, bp, b1, b2, gain, shift,
+    out, gres, gatt, gap, gbp, ga1, gb1, ga2, gb2,
+    act, slope, accs, gn2, res, n2s,
+):
+    r_p = jnp.zeros((512, 16), F32)
+    for g in range(4):
+        r_p += mm_nt(att[g], dp_[:, g * 256 : g * 256 + 256])
+    r_p = r_p.astype(BF)
+    for s in range(4):
+        cols = pl.ds(s * 256, 256)
+        val = mm(r_p, up[:, cols]) + bp[:, cols]
+        for g in range(4):
+            val += mm(att[g], wp[s, g * 256 : g * 256 + 256, :])
+        res[:, cols] = tok[:, cols].astype(F32) + val
+    xhat, inv = norm_parts(res[...])
+    n2 = (xhat * gain[...] + shift[...]).astype(BF)
+    n2s[...] = n2
+    r_1 = mm_nt(n2, d1[...]).astype(BF)
+
+    def up_step(i, carry):
+        s = i // 2
+        cols = pl.ds(pl.multiple_of(lax.rem(i, 2) * 512, 512), 512)
+        hid = mm(n2s[...], w1[s, :, cols]) + b1[i] + mm(r_1, u1[i])
+        cdf = 0.5 * (1.0 + lax.erf(hid * (0.5**0.5)))
+        act[i] = (hid * cdf).astype(BF)
+        slope[i] = cdf + hid * jnp.exp(-0.5 * hid * hid) * 0.3989422804014327
+        return carry
+
+    lax.fori_loop(0, 8, up_step, 0)
+    g_r2 = mm_nt(cot[...], u2[...]).astype(BF)
+    accs[...] = jnp.zeros_like(accs)
+    gn2[...] = jnp.zeros_like(gn2)
+
+    def down_step(i, carry):
+        r_2, g_r1 = carry
+        a = act[i]
+        r_2 += mm_nt(a, d2[i])
+        g = mm(g_r2, d2[i])
+        rows = pl.ds(pl.multiple_of(i * 512, 512), 512)
+        for s in range(4):
+            w = w2[s, rows, :]
+            accs[:, s * 256 : s * 256 + 256] += mm(a, w)
+            g += mm_nt(cot[:, s * 256 : s * 256 + 256], w)
+        gh = (g * slope[i]).astype(BF)
+        cols = pl.ds(pl.multiple_of(lax.rem(i, 2) * 512, 512), 512)
+        gn2[...] += mm_nt(gh, w1[i // 2, :, cols])
+        g_r1 += mm_nt(gh, u1[i])
+        ga2[i] = mm_tn(g_r2, a)
+        gb1[i] = mm_tn(r_1, gh)
+        return r_2, g_r1
+
+    r_2, g_r1 = lax.fori_loop(
+        0, 8, down_step, (jnp.zeros((512, 16), F32), jnp.zeros((512, 16), F32))
+    )
+    r_2, g_r1 = r_2.astype(BF), g_r1.astype(BF)
+    out[...] = (res[...] + accs[...] + b2[...] + mm(r_2, u2[...])).astype(BF)
+    gb2[...] = mm_tn(r_2, cot[...])
+    ga1[...] = mm_tn(g_r1, n2s[...])
+    g_n2 = gn2[...] + mm(g_r1, d1[...])
+    xhat, inv = norm_parts(res[...])
+    g_res = cot[...].astype(F32) + norm_back(g_n2, xhat, inv, gain[...])
+    gres[...] = g_res
+    gb = g_res.astype(BF)
+    g_rp = mm_nt(gb, up[...]).astype(BF)
+    gbp[...] = mm_tn(r_p, gb)
+    for g in range(4):
+        rows = pl.ds(g * 256, 256)
+        val = mm(g_rp, dp_[:, g * 256 : g * 256 + 256])
+        for s in range(4):
+            val += mm_nt(gb[:, s * 256 : s * 256 + 256], wp[s, rows, :])
+        gatt[g] = val.astype(BF)
+        gap[:, g * 256 : g * 256 + 256] = mm_tn(g_rp, att[g])
+
+
+def qkv_back_body(dq, dk, dv, tab, n1, red, wq, down, up6, parts, ga, gb6, gm):
+    gb_acc = [None] * 6
+    ga_acc = None
+    for slot in range(4):
+        cos, sin = tab[slot, :, :128], -tab[slot, :, 128:]
+        rows = pl.ds(slot * 512, 512)
+        first = 0 if slot < 2 else 2
+        g_red = jnp.zeros((512, 16), F32)
+        for role in range(first, 6):
+            cols = pl.ds((role % 2) * 256, 256)
+            if role < 2:
+                g = turn(dq[rows, cols], cos, sin)
+            elif role < 4:
+                g = turn(dk[rows, cols], cos, sin)
+            else:
+                g = dv[rows, cols]
+            g = g.astype(BF)
+            gm[role] = g
+            g_red += mm_nt(g, up6[role])
+            t = mm_tn(red[slot], g)
+            gb_acc[role] = t if gb_acc[role] is None else gb_acc[role] + t
+        g_red = g_red.astype(BF)
+        t = mm_tn(g_red, n1[slot])
+        ga_acc = t if ga_acc is None else ga_acc + t
+        total = mm(g_red, down[...])
+        for role in range(first, 6):
+            total += mm_nt(gm[role], wq[role])
+        parts[slot] = total
+    ga[...] = ga_acc
+    for role in range(6):
+        gb6[role] = gb_acc[role]
+
+
+def local_call(body, outs, scratch, *args):
+    vm = pl.BlockSpec(memory_space=pltpu.VMEM)
+    return pl.pallas_call(
+        body,
+        out_shape=outs,
+        in_specs=[vm] * len(args),
+        out_specs=[vm] * len(outs),
+        scratch_shapes=scratch,
+        compiler_params=pltpu.CompilerParams(vmem_limit_bytes=VM),
+    )(*args)
+
+
+def sds(shape, dtype):
+    return jax.ShapeDtypeStruct(shape, dtype)
+
+
+def rotary_table(places):
+    half = 10
+    freq = 10000.0 ** (-jnp.arange(half, dtype=F32) / half)
+    ang = places.astype(F32)[:, :, None] * freq
+    cos = [jnp.cos(ang[p]) for p in range(3)]
+    sin = [jnp.sin(ang[p]) for p in range(3)]
+    rest = places.shape[1:] + (HD - 60,)
+    c64 = jnp.concatenate([v for p in cos for v in (p, p)] + [jnp.ones(rest, F32)], axis=-1)
+    s64 = jnp.concatenate([v for p in sin for v in (-p, p)] + [jnp.zeros(rest, F32)], axis=-1)
+    return jnp.concatenate([c64, c64, s64, s64], axis=-1)
+
+
+SWAP = [(0, 1), (1, 0), (2, 3), (3, 2)]
+CROSS = [(0, 2), (2, 0), (1, 3), (3, 1)]
+
+
+def fast_shards(
+    nz, tokens, positions, adapter_index, qkv_weight, proj_weight, fc1_weight, fc2_weight,
+    vectors, fc1_bias, adapter_down, adapter_up, cotangent,
+):
+    seq = lax.axis_index("seq")
+    core = lax.rem(seq, 2)
+    tok4, _, wq, wp, w1, w2 = gather_all(
+        nz, tokens[0], qkv_weight, proj_weight, fc1_weight, fc2_weight
+    )
+    wq = wq.reshape(6, D, 256)
+    wp, w1, w2 = wp.reshape(4, D, 256), w1.reshape(4, D, 1024), w2.reshape(4, FF, 256)
+    vec = lax.all_gather(vectors, "seq", axis=1, tiled=True).astype(F32)
+    hb = lax.all_gather(fc1_bias, "seq", axis=0, tiled=True).astype(F32)
+    places = lax.all_gather(positions[:, 0], "seq", axis=1)
+    places = jnp.where(core == 1, jnp.stack([places[:, i] for i in (1, 0, 3, 2)], axis=1), places)
+    places = jnp.where(seq >= 2, jnp.stack([places[:, i] for i in (2, 3, 0, 1)], axis=1), places)
+    tab = rotary_table(places.reshape(3, 2048)).reshape(4, 512, 256)
+    index = lax.all_gather(adapter_index[:, 0], "dp", axis=0, tiled=True)
+    choose = index[:, None] == jnp.arange(NA, dtype=jnp.int32)[None, :]
+    mine = jnp.concatenate([adapter_down, adapter_up], axis=-1)
+    rk = mine.shape[1]
+    sel = jnp.sum(
+        jnp.where(choose[:, :, None, None], mine[None].astype(F32), 0.0), axis=1
+    ).astype(BF)
+    sel = lax.all_to_all(sel, "dp", 0, 0, tiled=True)
+    sel = sel.reshape(-1, sel.shape[-1])
+    sel = lax.all_gather(sel, "seq", axis=0)
+    nd = adapter_down.shape[-1]
+    down = jnp.moveaxis(sel[:, :, :nd], 0, 1).reshape(16, -1)
+    upm = jnp.moveaxis(sel[:, :, nd:], 0, 1).reshape(16, -1)
+    aq, ap, a1, a2 = down[:, :D], down[:, D : 2 * D], down[:, 2 * D : 3 * D], down[:, 3 * D :]
+    bq, bp_, b1_, b2_ = (
+        upm[:, : 3 * D], upm[:, 3 * D : 4 * D], upm[:, 4 * D : 4 * D + FF], upm[:, 4 * D + FF :],
+    )
+    up6 = lax.dynamic_index_in_dim(
+        jnp.moveaxis(bq.reshape(16, 6, 2, 256), 0, 2), core, 1, keepdims=False
+    )
+    bias6 = lax.dynamic_index_in_dim(
+        vec[4:7].reshape(6, 2, 1, 256), core, 1, keepdims=False
+    )
+    n1, red, q, k, v = local_call(
+        qkv_body,
+        [sds((4, 512, D), BF), sds((4, 512, 16), BF), sds((1024, 512), BF), sds((2048, 512), BF), sds((2048, 512), BF)],
+        [],
+        tok4, tab, wq, aq, up6, bias6, vec[0:1], vec[1:2],
+    )
+    o, lse = attend(q, k, v)
+    other = lax.ppermute(o[512:], "seq", SWAP)
+
+    def by_group(mine_, other_):
+        m, t = (
+            jnp.moveaxis(w.reshape(512, 2, 256), 1, 0) for w in (mine_, other_)
+        )
+        first = jnp.where(core == 0, m, t)
+        second = jnp.where(core == 0, t, m)
+        return jnp.stack([first[0], second[0], first[1], second[1]])
+
+    att = by_group(o[:512], other)
+    outs = local_call(
+        ffn_body,
+        [sds((512, D), BF), sds((512, D), F32), sds((4, 512, 256), BF),
+         sds((16, D), F32), sds((16, D), F32), sds((16, D), F32), sds((8, 16, 512), F32),
+         sds((8, 16, 512), F32), sds((16, D), F32)],
+        [pltpu.VMEM((8, 512, 512), BF), pltpu.VMEM((8, 512, 512), F32), pltpu.VMEM((512, D), F32),
+         pltpu.VMEM((512, D), F32), pltpu.VMEM((512, D), F32), pltpu.VMEM((512, D), BF)],
+        att, tokens[0], cotangent[0], wp, w1, w2,
+        ap, a1, jnp.moveaxis(a2.reshape(16, 8, 512), 1, 0),
+        bp_, jnp.moveaxis(b1_.reshape(16, 8, 512), 1, 0), b2_,
+        vec[7:8], hb.reshape(8, 1, 512), vec[8:9], vec[2:3], vec[3:4],
+    )
+    output, gres, gatt, gap, gbp, ga1, gb1, ga2, gb2 = outs
+    mine_ = jnp.where(core == 0, jnp.stack([gatt[0], gatt[2]]), jnp.stack([gatt[1], gatt[3]]))
+    send_ = jnp.where(core == 0, jnp.stack([gatt[1], gatt[3]]), jnp.stack([gatt[0], gatt[2]]))
+    other = lax.ppermute(send_, "seq", SWAP)
+    do = jnp.concatenate([mine_, other], axis=1)
+    do = jnp.moveaxis(do, 0, 1).reshape(1024, 512)
+    dq, dk, dv = attend_back(q, do, o, k, v, lse)
+    parts, gaq, gbq = local_call(
+        qkv_back_body,
+        [sds((4, 512, D), F32), sds((16, D), F32), sds((6, 16, 256), F32)],
+        [pltpu.VMEM((6, 512, 256), BF)],
+        dq, dk, dv, tab, n1, red, wq, aq, up6,
+    )
+    r13 = lax.ppermute(jnp.stack([parts[1], parts[3]]).astype(BF), "seq", SWAP)
+    r2 = lax.ppermute((parts[2] + r13[1].astype(F32)).astype(BF), "seq", CROSS)
+    g_n1 = parts[0] + r13[0].astype(F32) + r2.astype(F32)
+    xhat, inv = norm_parts(tokens[0].astype(F32))
+    input_grad = (gres + norm_back(g_n1, xhat, inv, vec[0:1])).astype(BF)
+    gbq_full = jnp.zeros((6, 2, 16, 256), F32)
+    gbq_full = lax.dynamic_update_index_in_dim(gbq_full, gbq[:, None], core, 1)
+    gbq_full = jnp.moveaxis(gbq_full, 2, 0).reshape(16, 3 * D)
+    flat8 = lambda w: jnp.moveaxis(w, 0, 1).reshape(16, FF)
+    cd = jnp.concatenate([gaq, gap, ga1, flat8(ga2)], axis=1).astype(BF)
+    cu = jnp.concatenate([gbq_full, gbp, flat8(gb1), gb2], axis=1).astype(BF)
+    cd = lax.psum_scatter(cd, "seq", scatter_dimension=1, tiled=True)
+    cu = lax.psum_scatter(cu, "seq", scatter_dimension=1, tiled=True)
+    both = jnp.concatenate([cd, cu], axis=1)
+    both = lax.all_to_all(both, "dp", 0, 0, tiled=True).reshape(-1, rk, both.shape[1])
+    grads = jnp.sum(
+        jnp.where(choose[:, :, None, None], both[:, None].astype(F32), 0.0), axis=0
+    )
+    return output[None], input_grad[None], grads[:, :, :nd], grads[:, :, nd:]
+
 
 def solution(mesh):
     in_specs = (
@@ -334,4 +1069,12 @@
         P(None, "dp", "seq"),
         P(None, "dp", "seq"),
     )
-    return jax.shard_map(shards, mesh=mesh, in_specs=in_specs, out_specs=out_specs, check_vma=False)
+    body = shards
+    if mesh.shape["seq"] == 4 and mesh.shape["dp"] % 2 == 0:
+
+        def body(tokens, *rest):
+            if tokens.shape[0] == 1 and tokens.shape[1] == 512:
+                return fast_shards(mesh.shape["dp"] // 2, tokens, *rest)
+            return shards(tokens, *rest)
+
+    return jax.shard_map(body, mesh=mesh, in_specs=in_specs, out_specs=out_specs, check_vma=False)

time: 1200 us -> 519 us (0.43)
  waiting for transfers between devices: 544 us -> 44.8 us
  Pallas kernels: 0 us -> 333 us
  matrix products: 306 us -> 0 us
  local copies, waits for them, and re-layouts: 201 us -> 47.2 us
  other arithmetic: 75.6 us -> 24.3 us
    all_gather x10 -> x0, waiting for transfers between devices: 348 us -> none  [the longest x4 210 us: fetch_weight(): return lax.all_gather(joined, 'dp', axis=0, tiled=True)]
    pallas_call x0 -> x6, Pallas kernels: none -> 333 us  [the longest x1 179 us: gather_all(): pl.pallas_call(functools.partial(gather_kernel, nz), out_shape=out, in_sp...]
    dot_general x90 -> x0, matrix products: 306 us -> none  [the longest x8 45.1 us: inner_step(): jnp.einsum('cqhd,ckhd->chqk', queries, key_block, preferred_element_type=...]
    reduce_scatter x5 -> x2, waiting for transfers between devices: 194 us -> 36.3 us  [the longest x1 23.4 us: fast_shards(): cu = lax.psum_scatter(cu, 'seq', scatter_dimension=1, tiled=True)]
    concatenate x4 -> x1, local copies, waits for them, and re-layouts: 76 us -> 16.7 us  [rotary_table(): return jnp.concatenate([c64, c64, s64, s64], axis=-1)]
    while x72 -> x0, local copies, waits for them, and re-layouts: 45.8 us -> none
    reduce_sum x14 -> x5, other arithmetic: 44.9 us -> 5.23 us  [the longest x1 2.98 us: norm_back(): jnp.mean(q, axis=-1, keepdims=True)]
    dynamic_update_slice x16 -> x1, local copies, waits for them, and re-layouts: 24.8 us -> 2.24 us  [fast_shards(): gbq_full = lax.dynamic_update_index_in_dim(gbq_full, gbq[:, None], core, 1)]
  transfers between devices with their start and end apart: 15 -> 8, of which waited for: 12 -> 4; matrix products, arithmetic and copies ran while one was open for 23% -> 10% of each run, Pallas kernels for 0% -> 35%
where the time goes in v1:
time: 519 us; the launch traced here: 512 us
  Pallas kernels  333 us (64%)
  local copies, waits for them, and re-layouts  47.2 us (9%)
  waiting for transfers between devices  44.8 us (9%)
  blocking collectives  36.4 us (7%)
  other arithmetic  24.3 us (5%)
  between operations  15.7 us (3%)
  starting transfers between devices  10.6 us (2%)
    pallas_call x1, Pallas kernels, gather_all(): pl.pallas_call(functools.partial(gather_kernel, nz), out_shape=out, in_sp...  179 us
    pallas_call x3, Pallas kernels, local_call(): pl.pallas_call(body, out_shape=outs, in_specs=[vm] * len(args), out_specs...  80.6 us
    pallas_call x1, Pallas kernels, attend_back(): pl.pallas_call(attend_back_body, grid=(4, nk // kb), in_specs=[full, full...  49.2 us
    pallas_call x1, Pallas kernels, attend(): pl.pallas_call(attend_body, grid=(4, nq // qb), in_specs=[pl.BlockSpec((q...  24 us
    reduce_scatter x1, waiting for transfers between devices, fast_shards(): cu = lax.psum_scatter(cu, 'seq', scatter_dimension=1, tiled=True)  23.4 us
    concatenate x1, local copies, waits for them, and re-layouts, rotary_table(): return jnp.concatenate([c64, c64, s64, s64], axis=-1)  16.7 us
    unnamed x1, blocking collectives  13.1 us
    reduce_scatter x1, waiting for transfers between devices, fast_shards(): cd = lax.psum_scatter(cd, 'seq', scatter_dimension=1, tiled=True)  12.9 us
  transfers between devices with their start and end apart: 8, of which 4 were waited for; matrix products, arithmetic and copies ran while one was open for 10% of the time, Pallas kernels for 35%

profile of v1, /device:TPU:0, one launch (start us, length us, event | category | flops | bytes accessed | tf_op | source)
XLA Modules:
  0.0 512.1 jit_solution(2130106200755337960)
XLA Ops:
  7.8 1.2 dynamic-slice.4
  9.7 13.1 %all-reduce = s32[8]{0:T(128)S(1)} all-reduce(s32[8]{0:T(128)S(1)} %bitcast_dynamic-update-slice_fusion), channel_id=2, replica_groups=mesh['dp'=8,'seq'=4] {'dp'}, use_global_device_ids=true, to_apply=%add | all-reduce | flops 8 | bytes 64
  24.1 1.4 select_reduce_fusion.1
  25.5 3.4 all-to-all-start
  29.6 5.2 %all_gather.15 = s32[3,4,512]{2,0,1:T(4,128)S(1)} all-gather(s32[3,1,512]{2,0,1:T(4,128)S(1)} %copy.46), channel_id=1, replica_groups=mesh['dp'=8,'seq'=4] {'seq'}, dimensions={1}, use_global_device_ids=true | all-gather | bytes 30720 | tf_op jit(solution)/shard_map/all_gather | solution.py:960
  35.8 11.8 %slice_sine_fusion = (f32[1,2048,10]{2,1,0:T(8,128)}, f32[1,2048,10]{2,1,0:T(8,128)}, f32[1,2048,10]{2,1,0:T(8,128)}, f32[1,2048,10]{2,1,0:T(8,128)S(1)}, f32[1,...) fusion(f32[3,2048,10]{2,1,0:T(8,128)S(1)} %broadcast_multiply_fusion), kind=kLoop, calls=%fused_computation.23 | loop fusion | bytes 737280 | tf_op jit(solution)/shard_map/sin | solution.py:936
  47.5 5.2 %all_gather.18 = bf16[9,1024]{1,0:T(8,128)(2,1)S(1)} all-gather(bf16[9,256]{1,0:T(8,128)(2,1)S(1)} %copy-done.14), channel_id=1, replica_groups=mesh['dp'=8,'seq'=4] {'seq'}, dimensions={1}, use_global_device_ids=true | all-gather | bytes 23040 | tf_op jit(solution)/shard_map/all_gather | solution.py:958
  53.4 2.4 neg.23
  55.7 1.1 neg.24
  57.9 179.3 %shard_map.147 = (bf16[4,512,1024]{2,1,0:T(8,128)(2,1)}, bf16[2,4,2,128,768]{4,3,2,1,0:T(8,128)(2,1)}, bf16[6,4,2,128,256]{4,3,2,1,0:T(8,128)(2,1)}, bf16[2,2,4,...) custom-call(bf16[512,1024]{1,0:T(8,128)(2,1)} %bitcast.77, ...), custom_call_target="tpu_custom_call" | custom-call | tf_op jit(solution)/shard_map/pallas_call | solution.py:643
  237.1 1.1 broadcast_in_dim.65
  239.2 16.7 %concatenate.28.tab = f32[4,512,256]{2,1,0:T(8,128)} concatenate(f32[4,512,10]{2,1,0:T(8,128)S(1)} %bitcast.87, f32[4,512,10]{2,1,0:T(8,128)S(1)} %bitcast.88, f32[4,512,10]{2,1,0:T(8,128)S(1)} %bitcast.83, f32[4,512,10]{2,1,0:T(8,128)S(1)} %bitcast.84, f32[4,512,10]{2,1,0:T(8,128)S(1)} %bitcast.79, f32[4,512,10]{2,1,0:T(8,128)S(1)} %bitcast.80, f32[4,512,4]{2,1,0:T(8,128)} %broadcast_in_dim.65, ...), dimensions={2} | concatenate | bytes 4194304 | tf_op jit(solution)/shard_map/concatenate | solution.py:940
  256.6 7.8 %all_gather.17 = bf16[4,16,4096]{2,1,0:T(8,128)(2,1)S(1)} all-gather(bf16[1,16,4096]{2,1,0:T(8,128)(2,1)S(1)} %all_gather_reshape.3), channel_id=1, replica_groups=mesh['dp'=8,'seq'=4] {'seq'}, dimensions={0}, use_global_device_ids=true | all-gather | bytes 655360 | tf_op jit(solution)/shard_map/all_gather | solution.py:973
  266.0 14.9 %shard_map.148 = (bf16[4,512,1024]{2,1,0:T(8,128)(2,1)}, bf16[4,512,16]{2,1,0:T(8,128)(2,1)}, bf16[1024,512]{1,0:T(8,128)(2,1)}, bf16[2048,512]{1,0:T(8,128)(2,1)}, bf16[2048,512]{1,0:T(8,128)(2,1)}) custom-call(bf16[4,512,1024]{2,1,0:T(8,128)(2,1)} %get-tuple-element.31.tok4, f32[4,512,256]{2,1,0:T(8,128)} %concatenate.28.tab, ...), custom_call_target="tpu_custom_call" | custom-call | tf_op jit(solution)/shard_map/pallas_call | solution.py:917
  280.9 24.0 %shard_map.149 = (bf16[1024,512]{1,0:T(8,128)(2,1)}, f32[4,2,1024]{2,1,0:T(2,128)}) custom-call(bf16[1024,512]{1,0:T(8,128)(2,1)} %get-tuple-element.33.q_ref, bf16[2048,512]{1,0:T(8,128)(2,1)} %get-tuple-element.34.k_ref, bf16[2048,512]{1,0:T(8,128)(2,1)} %get-tuple-element.35.v_ref), custom_call_target="tpu_custom_call" | custom-call | tf_op jit(solution)/shard_map/pallas_call | solution.py:714
  305.0 1.2 slice.163
  306.6 5.2 %all_gather.19 = bf16[4096]{0:T(1024)(128)(2,1)S(1)} all-gather(bf16[1024]{0:T(1024)(128)(2,1)S(1)} %copy-done.15), channel_id=1, replica_groups=mesh['dp'=8,'seq'=4] {'seq'}, dimensions={0}, use_global_device_ids=true | all-gather | bytes 10240 | tf_op jit(solution)/shard_map/all_gather | solution.py:959
  314.7 1.1 pad_maximum_fusion.1.att
  315.8 45.0 %shard_map.150 = (bf16[512,1024]{1,0:T(8,128)(2,1)}, f32[512,1024]{1,0:T(8,128)}, bf16[4,512,256]{2,1,0:T(8,128)(2,1)}, f32[16,1024]{1,0:T(8,128)}, f32[16,1024]...) custom-call(bf16[4,512,256]{2,1,0:T(8,128)(2,1)} %pad_maximum_fusion.1.a, ...), custom_call_target="tpu_custom_call" | custom-call | tf_op jit(solution)/shard_map/pallas_call | solution.py:917
  360.9 1.3 fusion.17
  362.8 1.5 collective-permute-done.1
  365.4 49.2 %shard_map.151 = (f32[1024,512]{1,0:T(8,128)}, f32[2048,512]{1,0:T(8,128)}, f32[2048,512]{1,0:T(8,128)}) custom-call(bf16[1024,512]{1,0:T(8,128)(2,1)} %get-tuple-element.33.q_ref, bf16[1024,512]{1,0:T(8,128)(2,1)} %bitcast.104, bf16[1024,512]{1,0:T(8,128)(2,1)} %get-tuple-element.36.o_ref, bf16[2048,512]{1,0:T(8,128)(2,1)} %get-tuple-element.34.k_ref, ...), custom_call_target="tpu_custom_call" | custom-call | tf_op jit(solution)/shard_map/pallas_call | solution.py:785
  414.6 20.6 %shard_map.152 = (f32[4,512,1024]{2,1,0:T(8,128)}, f32[16,1024]{1,0:T(8,128)}, f32[6,16,256]{2,1,0:T(8,128)}) custom-call(f32[1024,512]{1,0:T(8,128)} %get-tuple-element.44.dq, f32[2048,512]{1,0:T(8,128)} %get-tuple-element.45.dk, f32[2048,512]{1,0:T(8,128)} %get-tuple-element.46.dv, f32[4,512,256]{2,1,0:T(8,128)} %concatenate.28.tab, ...), custom_call_target="tpu_custom_call" | custom-call | tf_op jit(solution)/shard_map/pallas_call | solution.py:917
  435.3 4.0 convert.37
  441.5 2.2 dynamic_update_slice.4
  444.8 2.2 fusion.11
  447.5 12.9 %reduce-scatter.3.cloned.1.call-done = bf16[16,1792]{1,0:T(8,128)(2,1)} async-done(((bf16[16,7168]{1,0:T(8,128)(2,1)}), bf16[16,1792]{1,0:T(8,128)(2,1)}) %reduce-scatter.3.cloned.1.call-update) | async-done | bytes 57360 | tf_op jit(solution)/shard_map/reduce_scatter | solution.py:1041
  460.4 23.4 %reduce-scatter.5.cloned.1.call-done = bf16[16,2304]{1,0:T(8,128)(2,1)} async-done(((bf16[16,9216]{1,0:T(8,128)(2,1)}), bf16[16,2304]{1,0:T(8,128)(2,1)}) %reduce-scatter.5.cloned.1.call-update) | async-done | bytes 73744 | tf_op jit(solution)/shard_map/reduce_scatter | solution.py:1042
  485.5 5.5 %all-to-all-start.1 = ((bf16[8,2,4096]{2,1,0:T(2,128)(2,1)}), bf16[8,2,4096]{2,1,0:T(2,128)(2,1)S(1)}, u32[]{:S(2)}, u32[]{:S(2)}) async-start(bf16[8,2,4096]{2,1,0:T(2,128)(2,1)} %all_to_all.10), calls=%async_computation.3 | async-start | bytes 262144 | tf_op jit(solution)/shard_map/all_to_all | solution.py:1044
  491.4 6.9 %all-to-all-done.1 = bf16[8,2,4096]{2,1,0:T(2,128)(2,1)S(1)} async-done(((bf16[8,2,4096]{2,1,0:T(2,128)(2,1)}), bf16[8,2,4096]{2,1,0:T(2,128)(2,1)S(1)}, u32[]{:S(2)}, u32[]{:S(2)}) %all-to-all-start.1) | async-done | bytes 131104 | tf_op jit(solution)/shard_map/all_to_all | solution.py:1044
  500.1 3.0 fusion.14
  503.2 1.7 fusion.12
  (116 shorter events, 20.9 us)
Async XLA Ops:
  25.5 231.1 %all-to-all-start = ((bf16[8,2,4096]{2,1,0:T(2,128)(2,1)}), bf16[8,2,4096]{2,1,0:T(2,128)(2,1)S(1)}, u32[]{:S(2)}, u32[]{:S(2)}) async-start(bf16[8,2,4096]{2,1,0:T(2,128)(2,1)} %select_reduce_fusion.1), calls=%async_computation | async-start | bytes 262144 | tf_op jit(solution)/shard_map/all_to_all | solution.py:971
  28.9 431.6 %reduce-scatter.3.cloned.1.call-start = ((), (), s32[]{:S(2)}) async-start(), calls=%async_computation.4 | async-start | bytes 286720 | tf_op jit(solution)/shard_map/reduce_scatter | solution.py:1041
  35.7 11.8 %copy-start.14 = (bf16[9,256]{1,0:T(8,128)(2,1)S(1)}, bf16[9,256]{1,0:T(8,128)(2,1)}, u32[]{:S(2)}) copy-start(bf16[9,256]{1,0:T(8,128)(2,1)} %param.19) | copy-start | bytes 13828
  52.8 3.0 copy-start.2
  53.4 3.5 copy-start.1
  280.9 25.6 %copy-start.15 = (bf16[1024]{0:T(1024)(128)(2,1)S(1)}, bf16[1024]{0:T(1024)(128)(2,1)}, u32[]{:S(2)}) copy-start(bf16[1024]{0:T(1024)(128)(2,1)} %param.20) | copy-start | bytes 6148
  305.0 8.7 %copy-start.3 = (bf16[1024,512]{1,0:T(8,128)(2,1)S(1)}, bf16[1024,512]{1,0:T(8,128)(2,1)}, u32[]{:S(2)}) copy-start(bf16[1024,512]{1,0:T(8,128)(2,1)} %get-tuple-element.36.o_ref) | copy-start | bytes 3145732
  306.1 7.6 %collective-permute-start = (bf16[512,512]{1,0:T(8,128)(2,1)S(1)}, bf16[512,512]{1,0:T(8,128)(2,1)S(1)}, u32[]{:S(2)}, u32[]{:S(2)}) collective-permute-start(bf16[512,512]{1,0:T(8,128)(2,1)S(1)} %slice.163), channel_id=1, source_target_pairs={{0,1},{1,0},{2,3},{3,2},{4,5},{5,4},{6,7},{7,6},{8,9},{9,8},{10,11... | collective-permute-start | bytes 1572872 | tf_op jit(solution)/shard_map/ppermute | solution.py:994
  360.9 1.8 copy-start.6
  360.9 1.9 copy-start.11
  360.9 1.9 copy-start.10
  362.3 2.0 collective-permute-start.1
  439.5 1.0 copy-start.5
  439.5 1.0 copy-start.9
  439.5 1.0 copy-start.8
  439.5 1.0 copy-start.12
  439.5 1.8 copy-start.7
  439.8 4.8 copy-start
  439.8 5.0 collective-permute-start.2
  441.3 42.5 %reduce-scatter.5.cloned.1.call-start = ((), (), s32[]{:S(2)}) async-start(), calls=%async_computation.5 | async-start | bytes 368640 | tf_op jit(solution)/shard_map/reduce_scatter | solution.py:1042
  447.1 53.1 %copy-start.13 = (f32[1,1024]{1,0:T(1,128)S(1)}, f32[1,1024]{1,0:T(1,128)}, u32[]{:S(2)}) copy-start(f32[1,1024]{1,0:T(1,128)} %get-tuple-element.95.gain) | copy-start | bytes 12292
  447.1 53.1 %collective-permute-start.3 = (bf16[512,1024]{1,0:T(8,128)(2,1)S(1)}, bf16[512,1024]{1,0:T(8,128)(2,1)S(1)}, u32[]{:S(2)}, u32[]{:S(2)}) collective-permute-start(bf16[512,1024]{1,0:T(8,128)(2,1)S(1)} %fusion.11), channel_id=1, source_target_pairs={{0,2},{2,0},{1,3},{3,1},{4,6},{6,4},{5,7},{7,5},{8,10},{10,8},{9,1... | collective-permute-start | bytes 3145736 | tf_op jit(solution)/shard_map/ppermute | solution.py:1031
  485.5 12.9 %all-to-all-start.1 = ((bf16[8,2,4096]{2,1,0:T(2,128)(2,1)}), bf16[8,2,4096]{2,1,0:T(2,128)(2,1)S(1)}, u32[]{:S(2)}, u32[]{:S(2)}) async-start(bf16[8,2,4096]{2,1,0:T(2,128)(2,1)} %all_to_all.10), calls=%async_computation.3 | async-start | bytes 262144 | tf_op jit(solution)/shard_map/all_to_all | solution.py:1044
  500.1 3.0 copy-start.4
Sparse Core Ops, SparseCore 0:
  441.4 18.9 reduce-scatter.2
  463.5 20.2 reduce-scatter.4
